TPU v7x, 32 devices: a whole 2x2x4 slice. The times are simulated.
32 devices in a mesh: groups: 2 (over y), row: 4 (over z), col: 4 (over x, core), depth: 1.
Axes of the slice: x: 2, y: 2, z: 4, core: 2. Of those that a mesh axis runs over, the one named last changes fastest.
Arguments:
- mantissa: bfloat16 [1024, 8192], P(('groups', 'row', 'col'), 'depth'), parts along dimension 0, may hold values from -0.0625 to 0.0625
- exponent: int32 [1024], P(('groups', 'row', 'col')), parts along dimension 0, may hold values from -2 to 2
Outputs:
- kernel_gram: float32 [1024, 512], P(('groups', 'row'), ('col', 'depth')), parts along dimension 0
There are 2 independent parts, one for each index of `groups`. A program takes and returns all parts, laid end to end along the dimension named above; each array names one. Nothing has to cross between parts.
All inputs are finite; a program needn't handle non-finite values.
Results may differ from a plain program's by a relative error of at most 0.0003.
Values may be sent and summed in bfloat16 or wider, within the bound.
A program may use at most 64 MiB of HBM per device.

v0:
```python
import jax
import jax.numpy as jnp
from jax import lax
from jax.sharding import PartitionSpec as P


def broadcast(block, axis, source):
    block = jnp.where(lax.axis_index(axis) == source, block, jnp.zeros_like(block))
    return lax.psum(block, axis)


def product(left, right):
    return lax.dot_general(
        left, right, (((1,), (1,)), ((), ())), preferred_element_type=jnp.float32
    )


def shards(mantissa, exponent):
    scales = jnp.exp2(exponent.astype(jnp.float32))
    features = (mantissa.astype(jnp.float32) * scales[:, None]).astype(jnp.bfloat16)
    col_index = lax.axis_index("col")
    pieces_list = []
    rowblock = lax.all_gather(features, "col", axis=0, tiled=True)
    per_column = lax.axis_size("row") // lax.axis_size("col")
    for part_index in range(per_column):
        source_row = col_index * per_column + part_index
        column_block = broadcast(rowblock, "row", source_row)
        pieces_list.append(product(rowblock, column_block))
    partial_value = jnp.concatenate(pieces_list, axis=1)
    return lax.psum_scatter(partial_value, "depth", scatter_dimension=1, tiled=True)


def solution(mesh):
    in_specs = (P(("groups", "row", "col"), "depth"), P(("groups", "row", "col")))
    out_specs = P(("groups", "row"), ("col", "depth"))
    return jax.shard_map(shards, mesh=mesh, in_specs=in_specs, out_specs=out_specs, check_vma=False)
```

profile of v0, /device:TPU:0, one launch (start us, length us, event | category | flops | bytes accessed | tf_op | source)
XLA Modules:
  0.0 134.1 jit_solution(11146214375862392435)
XLA Ops:
  6.5 0.0 all-gather.2.cloned.1.call-start
  6.5 0.7 multiply_exponential_fusion
  7.2 2.0 %multiply_convert_fusion = bf16[32,8192]{1,0:T(8,128)(2,1)} fusion(bf16[32,8192]{1,0:T(8,128)(2,1)} %param.2, f32[32]{0:T(128)S(1)} %multiply_exponential_fusion), kind=kLoop, calls=%fused_computation.1 | loop fusion | flops 786432 | bytes 1048704 | tf_op jit(solution)/shard_map/convert_element_type | solution.py:20
  9.2 0.0 all-gather.2.cloned.1.call-update
  9.2 0.0 all-reduce.2.cloned.1.call-start
  9.3 25.4 %all-gather.2.cloned.1.call-done = bf16[128,8192]{1,0:T(8,128)(2,1)} async-done(((bf16[32,8192]{1,0:T(8,128)(2,1)}), bf16[128,8192]{1,0:T(8,128)(2,1)}) %all-gather.2.cloned.1.call-update) | async-done | bytes 2097168 | tf_op jit(solution)/shard_map/all_gather | solution.py:23
  34.7 3.1 %broadcast_select_fusion = bf16[128,8192]{1,0:T(8,128)(2,1)} fusion(bf16[128,8192]{1,0:T(8,128)(2,1)} %all-gather.2.cloned.1.call-done, pred[]{:T(512)S(6)} %eq.3), kind=kLoop, calls=%fused_computation | loop fusion | flops 1048576 | bytes 4194305 | tf_op jit(solution)/shard_map/jit(_where)/select_n | solution.py:8
  37.7 0.0 copy-start
  37.7 0.0 all-reduce.2.cloned.1.call-update
  37.7 86.6 %all-reduce.2.cloned.1.call-done = bf16[128,8192]{1,0:T(8,128)(2,1)} async-done(((bf16[128,8192]{1,0:T(8,128)(2,1)}), bf16[128,8192]{1,0:T(8,128)(2,1)}) %all-reduce.2.cloned.1.call-update) | async-done | bytes 2097168 | tf_op jit(solution)/shard_map/psum | solution.py:9
  124.3 0.0 copy-done
  124.3 2.9 %fusion = f32[128,128]{1,0:T(8,128)} fusion(bf16[128,8192]{1,0:T(8,128)(2,1)S(1)} %copy-done, bf16[128,8192]{1,0:T(8,128)(2,1)} %all-reduce.2.cloned.1.call-done), kind=kOutput, calls=%fused_computation.3 | convolution fusion | flops 268435456 | bytes 4259840 | tf_op jit(solution)/shard_map/dot_general | solution.py:13
Async XLA Ops:
  6.5 28.1 %all-gather.2.cloned.1.call-start = ((), (), s32[]{:S(2)}) async-start(), calls=%async_computation | async-start | bytes 2621440 | tf_op jit(solution)/shard_map/all_gather | solution.py:23
  9.2 115.1 %all-reduce.2.cloned.1.call-start = ((), (), s32[]{:S(2)}) async-start(), calls=%async_computation.1 | async-start | bytes 4194304 | tf_op jit(solution)/shard_map/psum | solution.py:9
  37.7 86.6 %copy-start = (bf16[128,8192]{1,0:T(8,128)(2,1)S(1)}, bf16[128,8192]{1,0:T(8,128)(2,1)}, u32[]{:S(2)}) copy-start(bf16[128,8192]{1,0:T(8,128)(2,1)} %all-gather.2.cloned.1.call-done) | copy-start | bytes 6291460
Sparse Core Ops, SparseCore 0:
  9.3 25.2 all-gather.1
  37.9 86.3 all-reduce.1
where the time goes:
time: 134 us
  waiting for transfers between devices  112 us (84%)
  between operations  13.4 us (10%)
  other arithmetic  5.7 us (4%)
  matrix products  2.93 us (2%)
    psum x1, waiting for transfers between devices, broadcast(): return lax.psum(block, axis)  86.6 us
    all_gather x1, waiting for transfers between devices, shards(): rowblock = lax.all_gather(features, 'col', axis=0, tiled=True)  25.4 us
    select_n x1, other arithmetic, broadcast(): jnp.where(lax.axis_index(axis) == source, block, jnp.zeros_like(block))  3.05 us
    dot_general x1, matrix products, product(): lax.dot_general(left, right, (((1,), (1,)), ((), ())), preferred_element_...  2.93 us
  transfers between devices with their start and end apart: 2, of which 2 were waited for; matrix products, arithmetic and copies ran while one was open for 0% of the time, Pallas kernels for 0%

commit v1 on v0

v1 whole, which is shorter than its diff:
```python
import functools

import jax
import jax.numpy as jnp
from jax import lax
from jax.experimental import pallas as pl
from jax.experimental.pallas import tpu as pltpu
from jax.sharding import PartitionSpec as P

CHUNKS = 4
MESH = pl.DeviceIdType.MESH


def held_upper(rows, z, b):
    ordinary = (b >= 1) & (b <= z) & jnp.logical_not((z == rows - 1) & (b == 1))
    return ordinary | ((z == rows - 2) & (b == rows - 1))


def held_lower(rows, z, b):
    return held_upper(rows, rows - 1 - z, b)


def worked(rows, z, b):
    return held_upper(rows, z, b) | held_lower(rows, z, rows - b)


def scale_of(exponent):
    size = jnp.abs(exponent)
    up = jnp.ones(exponent.shape, jnp.float32)
    down = up
    for bit in range(7):
        is_set = ((size >> bit) & 1) == 1
        up = jnp.where(is_set, up * 2.0 ** (2**bit), up)
        down = jnp.where(is_set, down * 2.0 ** -(2**bit), down)
    return jnp.where(exponent < 0, down, up)


def kernel(rows, cols, depths, mantissa, exponent, out, raw, tile, upper, lower, acc_a, acc_b, sums, direct, mirror,
           load_sem, plane_send, plane_recv, up_send, up_recv, down_send, down_recv, extra_send,
           direct_send, direct_recv, mirror_send, mirror_recv):
    z, c, d = lax.axis_index("row"), lax.axis_index("col"), lax.axis_index("depth")
    n, features = raw.shape
    size = n * cols
    half = features // 2
    width = half // CHUNKS
    q = c * depths + d

    load = pltpu.make_async_copy(mantissa, raw, load_sem)
    load.start()

    barrier = pltpu.get_barrier_semaphore()

    def greet(k, _):
        there = {"row": k // (cols * depths), "col": (k // depths) % cols, "depth": k % depths}

        @pl.when(k != z * cols * depths + q)
        def _():
            pl.semaphore_signal(barrier, inc=1, device_id=there, device_id_type=MESH)

        return 0

    lax.fori_loop(0, rows * cols * depths, greet, 0)

    wide = jnp.broadcast_to(exponent[...].reshape(1, n), (n, n))
    eye = lax.broadcasted_iota(jnp.int32, (n, n), 0) == lax.broadcasted_iota(jnp.int32, (n, n), 1)
    scale = scale_of(jnp.sum(jnp.where(eye, wide, 0), axis=1, keepdims=True))
    load.wait()
    own_rows = pl.ds(pl.multiple_of(c * n, n), n)
    for i in range(2 * CHUNKS):
        piece = pl.ds(i * width, width)
        scaled = (raw[:, piece].astype(jnp.float32) * scale).astype(jnp.bfloat16)
        tile[own_rows, piece] = scaled
        if i < CHUNKS:
            upper[pl.ds(0, n), piece] = scaled
        else:
            lower[pl.ds(0, n), pl.ds((i - CHUNKS) * width, width)] = scaled
    pl.semaphore_wait(barrier, rows * cols * depths - 1)

    def plane_copy(rel, bit, chunk):
        block = tile.at[pl.ds(pl.multiple_of((c ^ rel) * n, n), n), pl.ds(chunk * width, width)]
        return pltpu.make_async_remote_copy(
            src_ref=block, dst_ref=block, send_sem=plane_send.at[rel | bit, chunk],
            recv_sem=plane_recv.at[rel | bit, chunk], device_id={"col": c ^ bit}, device_id_type=MESH)

    def lower_bits(rel):
        bit = (rel & -rel if rel else cols) >> 1
        while bit:
            yield bit
            bit >>= 1

    def plane_start(rel, chunk):
        for bit in lower_bits(rel):
            plane_copy(rel, bit, chunk).start()

    def plane_arrived(rel, chunk):
        block = tile.at[pl.ds(pl.multiple_of((c ^ rel) * n, n), n), pl.ds(chunk * width, width)]
        pltpu.make_async_copy(block, block, plane_recv.at[rel, chunk]).wait()

    def line_copy(buffer, send, recv, there, b, i):
        piece = pl.ds(i * width, width)
        return pltpu.make_async_remote_copy(
            src_ref=buffer.at[pl.ds(b * n, n), piece], dst_ref=buffer.at[pl.ds((b + 1) * n, n), piece],
            send_sem=send.at[b, i], recv_sem=recv.at[b + 1, i], device_id={"row": there}, device_id_type=MESH)

    def extra_copy(buffer, recv, there, i):
        piece = pl.ds(i * width, width)
        return pltpu.make_async_remote_copy(
            src_ref=buffer.at[pl.ds(0, n), piece], dst_ref=buffer.at[pl.ds((rows - 1) * n, n), piece],
            send_sem=extra_send.at[i], recv_sem=recv.at[rows - 1, i], device_id={"row": there}, device_id_type=MESH)

    def line_arrived(buffer, recv, b, i):
        block = buffer.at[pl.ds(b * n, n), pl.ds(i * width, width)]
        pltpu.make_async_copy(block, block, recv.at[b, i]).wait()

    m = rows - 1 - z
    for i in range(CHUNKS):
        @pl.when(z < rows - 2)
        def _():
            line_copy(upper, up_send, up_recv, z + 1, 0, i).start()

        @pl.when(z > 1)
        def _():
            line_copy(lower, down_send, down_recv, z - 1, 0, i).start()

        plane_start(0, i)
        plane_start(0, CHUNKS + i)

    for i in range(CHUNKS):
        @pl.when(z == 0)
        def _():
            line_copy(upper, up_send, up_recv, z + 1, 0, i).wait_send()
            extra_copy(lower, down_recv, z + 1, i).start()

        @pl.when(z == rows - 1)
        def _():
            line_copy(lower, down_send, down_recv, z - 1, 0, i).wait_send()
            extra_copy(upper, up_recv, z - 1, i).start()

    def arrive(b, i):
        @pl.when(held_upper(rows, z, b))
        def _():
            line_arrived(upper, up_recv, b, i)

        @pl.when(held_lower(rows, z, b))
        def _():
            line_arrived(lower, down_recv, b, i)

        if b < rows - 1:
            @pl.when((b <= z) & (z < rows - 1))
            def _():
                line_copy(upper, up_send, up_recv, z + 1, b, i).start()

            @pl.when((b <= m) & (m < rows - 1))
            def _():
                line_copy(lower, down_send, down_recv, z - 1, b, i).start()

    def plane_arrive(chunk):
        for bit in reversed(range(cols.bit_length() - 1)):
            for rel in range(1 << bit, cols, 1 << (bit + 1)):
                plane_arrived(rel, chunk)
                plane_start(rel, chunk)

    for b in range(1, rows - 2):
        for i in range(CHUNKS):
            arrive(b, i)
            if b == rows - 3 and i % 2 == 1:
                plane_arrive(i // 2)
                plane_arrive(CHUNKS + i // 2)

    dims = (((1,), (1,)), ((), ()))
    for i in range(CHUNKS):
        arrive(rows - 2, i)
        if i >= CHUNKS // 2:
            plane_arrive(i)
            plane_arrive(CHUNKS + i)
        arrive(rows - 1, i)
        piece, other = pl.ds(i * width, width), pl.ds(half + i * width, width)
        term_a = lax.dot_general(upper[:, piece], tile[:, piece], dims, preferred_element_type=jnp.float32)
        term_b = lax.dot_general(lower[:, piece], tile[:, other], dims, preferred_element_type=jnp.float32)
        if i == 0:
            acc_a[...] = term_a
            acc_b[...] = term_b
        else:
            acc_a[...] += term_a
            acc_b[...] += term_b

    def place(row, tile_index):
        return {"row": row, "col": tile_index // depths, "depth": tile_index % depths}

    stripe = pl.ds(pl.multiple_of(c * n, n), n)

    def direct_copy(b, j):
        return pltpu.make_async_remote_copy(
            src_ref=sums.at[b], dst_ref=direct.at[d, stripe], send_sem=direct_send.at[b],
            recv_sem=direct_recv.at[d, c], device_id=place(z, j), device_id_type=MESH)

    def mirror_copy(b, j):
        return pltpu.make_async_remote_copy(
            src_ref=sums.at[b], dst_ref=mirror.at[d, stripe], send_sem=mirror_send.at[b],
            recv_sem=mirror_recv.at[d, c], device_id=place(j, z), device_id_type=MESH)

    for b in range(1, rows):
        j = lax.rem(z - b + rows, rows)

        @pl.when(worked(rows, z, b))
        def _():
            first = jnp.where(held_upper(rows, z, b), acc_a[pl.ds(b * n, n), :], 0.0)
            second = jnp.where(held_lower(rows, z, rows - b), acc_b[pl.ds((rows - b) * n, n), :], 0.0)
            sums[b] = first + second
            mirror_copy(b, j).start()

            @pl.when(j != q)
            def _():
                direct_copy(b, j).start()

            @pl.when(j == q)
            def _():
                direct[d, stripe] = sums[b]

    sums[0] = acc_a[pl.ds(0, n), :] + acc_b[pl.ds(0, n), :]

    @pl.when(z != q)
    def _():
        mirror_copy(0, z).start()

    @pl.when(z == q)
    def _():
        mirror[d, stripe] = sums[0]

    for b in range(rows):
        for i in range(CHUNKS):
            if b < rows - 1:
                @pl.when((b <= z) & (z < rows - 1) & jnp.logical_not((b == 0) & ((z == rows - 2) | (z == 0))))
                def _():
                    line_copy(upper, up_send, up_recv, z + 1, b, i).wait_send()

                @pl.when((b <= m) & (m < rows - 1) & jnp.logical_not((b == 0) & ((m == rows - 2) | (m == 0))))
                def _():
                    line_copy(lower, down_send, down_recv, z - 1, b, i).wait_send()

    for i in range(CHUNKS):
        @pl.when((z == 0) | (z == rows - 1))
        def _():
            extra_copy(lower, down_recv, 1, i).wait_send()

    for chunk in range(2 * CHUNKS):
        for rel in range(cols):
            for bit in lower_bits(rel):
                plane_copy(rel, bit, chunk).wait_send()

    def wait_block(buffer, recv, cc, dd):
        block = buffer.at[dd, pl.ds(cc * n, n)]
        pltpu.make_async_copy(block, block, recv.at[dd, cc]).wait()

    has_direct = (z != q) & worked(rows, z, lax.rem(z - q + rows, rows))
    has_mirror = (z == q) | worked(rows, q, lax.rem(q - z + rows, rows))

    def gathered(buffer):
        total = buffer[0]
        for dd in range(1, depths):
            total = total + buffer[dd]
        return total

    @pl.when(has_direct)
    def _():
        for dd in range(depths):
            for cc in range(cols):
                @pl.when((cc != c) | (dd != d))
                def _():
                    wait_block(direct, direct_recv, cc, dd)

        out[...] = gathered(direct).T

    @pl.when(has_mirror)
    def _():
        for dd in range(depths):
            for cc in range(cols):
                @pl.when((z != q) | (cc != c) | (dd != d))
                def _():
                    wait_block(mirror, mirror_recv, cc, dd)

        total = gathered(mirror)

        @pl.when(has_direct)
        def _():
            out[...] += total

        @pl.when(jnp.logical_not(has_direct))
        def _():
            out[...] = total

    for b in range(rows):
        j = lax.rem(z - b + rows, rows)
        if b:
            @pl.when(worked(rows, z, b))
            def _():
                mirror_copy(b, j).wait_send()

                @pl.when(j != q)
                def _():
                    direct_copy(b, j).wait_send()
        else:
            @pl.when(z != q)
            def _():
                mirror_copy(0, z).wait_send()


def shards(rows, cols, depths, mantissa, exponent):
    n, features = mantissa.shape
    size = n * cols
    half = features // 2
    dma = pltpu.SemaphoreType.DMA
    return pl.pallas_call(
        functools.partial(kernel, rows, cols, depths),
        out_shape=jax.ShapeDtypeStruct((size, size), jnp.float32),
        in_specs=[pl.BlockSpec(memory_space=pl.ANY), pl.BlockSpec(memory_space=pltpu.VMEM)],
        out_specs=pl.BlockSpec(memory_space=pltpu.VMEM),
        scratch_shapes=[
            pltpu.VMEM((n, features), jnp.bfloat16),
            pltpu.VMEM((size, features), jnp.bfloat16),
            pltpu.VMEM((rows * n, half), jnp.bfloat16),
            pltpu.VMEM((rows * n, half), jnp.bfloat16),
            pltpu.VMEM((rows * n, size), jnp.float32),
            pltpu.VMEM((rows * n, size), jnp.float32),
            pltpu.VMEM((rows, n, size), jnp.float32),
            pltpu.VMEM((depths, size, size), jnp.float32),
            pltpu.VMEM((depths, size, size), jnp.float32),
            dma,
            dma((cols, 2 * CHUNKS)), dma((cols, 2 * CHUNKS)),
            dma((rows, CHUNKS)), dma((rows, CHUNKS)),
            dma((rows, CHUNKS)), dma((rows, CHUNKS)),
            dma((CHUNKS,)),
            dma((rows,)), dma((depths, cols)),
            dma((rows,)), dma((depths, cols)),
        ],
        compiler_params=pltpu.CompilerParams(
            collective_id=0, has_side_effects=True, vmem_limit_bytes=48 * 2**20),
    )(mantissa, exponent)


def solution(mesh):
    rows, cols, depths = (mesh.shape[axis] for axis in ("row", "col", "depth"))
    assert rows >= 3 and cols & (cols - 1) == 0 and rows == cols * depths
    in_specs = (P(("groups", "row", "col"), "depth"), P(("groups", "row", "col")))
    out_specs = P(("groups", "row"), ("col", "depth"))
    return jax.shard_map(
        functools.partial(shards, rows, cols, depths), mesh=mesh, in_specs=in_specs, out_specs=out_specs, check_vma=False)
```

time: 134 us -> 32.3 us (0.24)
  waiting for transfers between devices: 112 us -> 0 us
  Pallas kernels: 0 us -> 29.8 us
  between operations: 13.4 us -> 0.01 us
  other arithmetic: 5.7 us -> 0 us
  matrix products: 2.93 us -> 0 us
  local copies, waits for them, and re-layouts: 0.01 us -> 2.33 us
    psum x1 -> x0, waiting for transfers between devices: 86.6 us -> none  [broadcast(): return lax.psum(block, axis)]
    pallas_call x0 -> x1, Pallas kernels: none -> 29.8 us  [shards(): pl.pallas_call(functools.partial(kernel, rows, cols, depths), out_shape=j...]
    all_gather x1 -> x0, waiting for transfers between devices: 25.4 us -> none  [shards(): rowblock = lax.all_gather(features, 'col', axis=0, tiled=True)]
    select_n x1 -> x0, other arithmetic: 3.05 us -> none  [broadcast(): jnp.where(lax.axis_index(axis) == source, block, jnp.zeros_like(block))]
    dot_general x1 -> x0, matrix products: 2.93 us -> none  [product(): lax.dot_general(left, right, (((1,), (1,)), ((), ())), preferred_element_...]
    unnamed x2 -> x5, local copies, waits for them, and re-layouts: 0.01 us -> 2.33 us
    convert_element_type x1 -> x0, other arithmetic: 1.99 us -> none  [shards(): (mantissa.astype(jnp.float32) * scales[:, None]).astype(jnp.bfloat16)]
  transfers between devices with their start and end apart: 2 -> 0, of which waited for: 2 -> 0; matrix products, arithmetic and copies ran while one was open for 0% -> 0% of each run, Pallas kernels for 0% -> 0%
where the time goes in v1:
time: 32.3 us; the launch traced here: 32.1 us
  Pallas kernels  29.8 us (92%)
  local copies, waits for them, and re-layouts  2.33 us (7%)
    pallas_call x1, Pallas kernels, shards(): pl.pallas_call(functools.partial(kernel, rows, cols, depths), out_shape=j...  29.8 us
    unnamed x5, local copies, waits for them, and re-layouts  2.33 us

profile of v1, /device:TPU:0, one launch (start us, length us, event | category | flops | bytes accessed | tf_op | source)
XLA Modules:
  0.0 32.1 jit_solution(15596706945038834840)
XLA Ops:
  0.0 0.0 copy-start
  0.0 1.0 %copy-done = bf16[32,8192]{1,0:T(8,128)(2,1)S(1)} copy-done((bf16[32,8192]{1,0:T(8,128)(2,1)S(1)}, bf16[32,8192]{1,0:T(8,128)(2,1)}, u32[]{:S(2)}) %copy-start) | copy-done | bytes 524312
  1.0 0.0 copy-start.1
  1.0 0.7 %copy-done.1 = s32[32]{0:T(128)S(1)} copy-done((s32[32]{0:T(128)S(1)}, s32[32]{0:T(128)}, u32[]{:S(2)}) %copy-start.1) | copy-done | bytes 152
  1.7 29.8 %shard_map.28 = f32[128,128]{1,0:T(8,128)S(1)} custom-call(bf16[32,8192]{1,0:T(8,128)(2,1)S(1)} %copy-done, s32[32]{0:T(128)S(1)} %copy-done.1), custom_call_target="tpu_custom_call" | custom-call | tf_op jit(solution)/shard_map/pallas_call | solution.py:313
  31.5 0.6 %copy.4 = f32[128,128]{1,0:T(8,128)} copy(f32[128,128]{1,0:T(8,128)S(1)} %shard_map.28) | data formatting | bytes 131072
Async XLA Ops:
  0.0 1.0 %copy-start = (bf16[32,8192]{1,0:T(8,128)(2,1)S(1)}, bf16[32,8192]{1,0:T(8,128)(2,1)}, u32[]{:S(2)}) copy-start(bf16[32,8192]{1,0:T(8,128)(2,1)} %mantissa.1) | copy-start | bytes 1572868
  1.0 0.7 %copy-start.1 = (s32[32]{0:T(128)S(1)}, s32[32]{0:T(128)}, u32[]{:S(2)}) copy-start(s32[32]{0:T(128)} %exponent.1) | copy-start | bytes 388

commit v2 on v1

v2 whole, which is shorter than its diff:
```python
import functools

import jax
import jax.numpy as jnp
from jax import lax
from jax.experimental import pallas as pl
from jax.experimental.pallas import tpu as pltpu
from jax.sharding import PartitionSpec as P

CHUNKS = 4
PLANE = 2
LAG = 3
MESH = pl.DeviceIdType.MESH


def held_upper(rows, z, b):
    ordinary = (b >= 1) & (b <= z) & jnp.logical_not((z == rows - 1) & (b == 1))
    return ordinary | ((z == rows - 2) & (b == rows - 1))


def held_lower(rows, z, b):
    return held_upper(rows, rows - 1 - z, b)


def worked(rows, z, b):
    return held_upper(rows, z, b) | held_lower(rows, z, rows - b)


def scale_of(exponent):
    size = jnp.abs(exponent)
    up = jnp.ones(exponent.shape, jnp.float32)
    down = up
    for bit in range(7):
        is_set = ((size >> bit) & 1) == 1
        up = jnp.where(is_set, up * 2.0 ** (2**bit), up)
        down = jnp.where(is_set, down * 2.0 ** -(2**bit), down)
    return jnp.where(exponent < 0, down, up)


def kernel(rows, cols, depths, mantissa, exponent, out, raw, powers, tile, upper, lower, acc_a, acc_b, sums, direct, mirror,
           load_sem, power_sem, plane_send, plane_recv, up_send, up_recv, down_send, down_recv, extra_send,
           direct_send, direct_recv, mirror_send, mirror_recv):
    z, c, d = lax.axis_index("row"), lax.axis_index("col"), lax.axis_index("depth")
    n, features = raw.shape
    size = n * cols
    half = features // 2
    width = half // CHUNKS
    q = c * depths + d

    def load(half_index, i):
        piece = pl.ds(half_index * half + i * width, width)
        return pltpu.make_async_copy(mantissa.at[:, piece], raw.at[:, piece], load_sem.at[half_index, i])

    for i in range(CHUNKS):
        for half_index in range(2):
            load(half_index, i).start()
    load_powers = pltpu.make_async_copy(exponent, powers, power_sem)
    load_powers.start()

    barrier = pltpu.get_barrier_semaphore()

    def greet(k, _):
        @pl.when(k != q)
        def _():
            there = {"col": k // depths, "depth": k % depths}
            pl.semaphore_signal(barrier, inc=1, device_id=there, device_id_type=MESH)

        return 0

    lax.fori_loop(0, cols * depths, greet, 0)

    @pl.when(z > 0)
    def _():
        pl.semaphore_signal(barrier, inc=1, device_id={"row": z - 1}, device_id_type=MESH)

    @pl.when(z < rows - 1)
    def _():
        pl.semaphore_signal(barrier, inc=1, device_id={"row": z + 1}, device_id_type=MESH)

    load_powers.wait()
    wide = jnp.broadcast_to(powers[...].reshape(1, n), (n, n))
    eye = lax.broadcasted_iota(jnp.int32, (n, n), 0) == lax.broadcasted_iota(jnp.int32, (n, n), 1)
    scale = scale_of(jnp.sum(jnp.where(eye, wide, 0), axis=1, keepdims=True))
    own_rows = pl.ds(pl.multiple_of(c * n, n), n)

    def scaled(half_index, i, block):
        load(half_index, i).wait()
        piece = pl.ds(half_index * half + i * width, width)
        value = (raw[:, piece].astype(jnp.float32) * scale).astype(jnp.bfloat16)
        tile[own_rows, piece] = value
        block[pl.ds(0, n), pl.ds(i * width, width)] = value

    span = half // PLANE

    def plane_block(rel, t):
        start = t % 2 * half + t // 2 * span
        return tile.at[pl.ds(pl.multiple_of((c ^ rel) * n, n), n), pl.ds(start, span)]

    def plane_copy(rel, bit, t):
        block = plane_block(rel, t)
        return pltpu.make_async_remote_copy(
            src_ref=block, dst_ref=block, send_sem=plane_send.at[rel | bit],
            recv_sem=plane_recv.at[rel | bit, t], device_id={"col": c ^ bit}, device_id_type=MESH)

    def lower_bits(rel):
        bit = (rel & -rel if rel else cols) >> 1
        while bit:
            yield bit
            bit >>= 1

    def plane_arrivals(t):
        for bit in reversed(range(cols.bit_length() - 1)):
            for rel in range(1 << bit, cols, 1 << (bit + 1)):
                block = plane_block(rel, t)
                pltpu.make_async_copy(block, block, plane_recv.at[rel, t]).wait()
                for low in lower_bits(rel):
                    plane_copy(rel, low, t).start()

    def line_copy(buffer, send, recv, there, b, i):
        piece = pl.ds(i * width, width)
        return pltpu.make_async_remote_copy(
            src_ref=buffer.at[pl.ds(b * n, n), piece], dst_ref=buffer.at[pl.ds((b + 1) * n, n), piece],
            send_sem=send.at[b], recv_sem=recv.at[b + 1, i], device_id={"row": there}, device_id_type=MESH)

    def extra_copy(buffer, recv, there, i):
        piece = pl.ds(i * width, width)
        return pltpu.make_async_remote_copy(
            src_ref=buffer.at[pl.ds(0, n), piece], dst_ref=buffer.at[pl.ds((rows - 1) * n, n), piece],
            send_sem=extra_send, recv_sem=recv.at[rows - 1, i], device_id={"row": there}, device_id_type=MESH)

    def line_arrived(buffer, recv, b, i):
        block = buffer.at[pl.ds(b * n, n), pl.ds(i * width, width)]
        pltpu.make_async_copy(block, block, recv.at[b, i]).wait()

    m = rows - 1 - z

    def line_sends(t):
        b, i = divmod(t, CHUNKS)

        @pl.when((z < rows - 2) & (b <= z))
        def _():
            line_copy(upper, up_send, up_recv, z + 1, b, i).start()

        @pl.when((m < rows - 2) & (b <= m))
        def _():
            line_copy(lower, down_send, down_recv, z - 1, b, i).start()

        if b == 1:
            @pl.when(z == 0)
            def _():
                extra_copy(lower, down_recv, z + 1, i).start()

            @pl.when(m == 0)
            def _():
                extra_copy(upper, up_recv, z - 1, i).start()

    def line_arrivals(t):
        b, i = divmod(t, CHUNKS)
        b += 1

        @pl.when((b <= z) & (z <= rows - 2))
        def _():
            line_arrived(upper, up_recv, b, i)

            @pl.when(z == rows - 2)
            def _():
                line_copy(upper, up_send, up_recv, z + 1, b, i).start()

        @pl.when((b <= m) & (m <= rows - 2))
        def _():
            line_arrived(lower, down_recv, b, i)

            @pl.when(m == rows - 2)
            def _():
                line_copy(lower, down_send, down_recv, z - 1, b, i).start()

    def last_arrivals(i):
        @pl.when(z == rows - 2)
        def _():
            line_arrived(upper, up_recv, rows - 1, i)

        @pl.when(m == rows - 2)
        def _():
            line_arrived(lower, down_recv, rows - 1, i)

        @pl.when(z == rows - 1)
        def _():
            for b in range(2, rows):
                line_arrived(upper, up_recv, b, i)

        @pl.when(m == rows - 1)
        def _():
            for b in range(2, rows):
                line_arrived(lower, down_recv, b, i)

    dims = (((1,), (1,)), ((), ()))

    def multiply(i):
        piece, other = pl.ds(i * width, width), pl.ds(half + i * width, width)
        term_a = lax.dot_general(upper[:, piece], tile[:, piece], dims, preferred_element_type=jnp.float32)
        term_b = lax.dot_general(lower[:, piece], tile[:, other], dims, preferred_element_type=jnp.float32)
        if i == 0:
            acc_a[...] = term_a
            acc_b[...] = term_b
        else:
            acc_a[...] += term_a
            acc_b[...] += term_b

    line_steps = (rows - 2) * CHUNKS
    plane_done = 0
    for step in range(line_steps + LAG):
        if step < CHUNKS:
            scaled(0, step, upper)
            scaled(1, step, lower)
        if step == 0:
            pl.semaphore_wait(barrier, cols * depths + 1 - jnp.where((z == 0) | (z == rows - 1), 1, 0))
        if step < line_steps:
            line_sends(step)
        per_span = CHUNKS // PLANE
        if step < CHUNKS and step % per_span == per_span - 1:
            for t in (step // per_span * 2, step // per_span * 2 + 1):
                for bit in lower_bits(0):
                    plane_copy(0, bit, t).start()
        done = step - LAG
        if done >= 0:
            line_arrivals(done)
            i = done - (rows - 3) * CHUNKS
            due = min((done + 1) // per_span, 2 * PLANE)
            if i >= 0:
                due = max(due, i // per_span * 2 + 2)
            for t in range(plane_done, due):
                plane_arrivals(t)
            plane_done = due
            if i >= 0:
                last_arrivals(i)
                multiply(i)

    def place(row, tile_index):
        return {"row": row, "col": tile_index // depths, "depth": tile_index % depths}

    stripe = pl.ds(pl.multiple_of(c * n, n), n)

    def direct_copy(b, j):
        return pltpu.make_async_remote_copy(
            src_ref=sums.at[b], dst_ref=direct.at[d, stripe], send_sem=direct_send.at[b],
            recv_sem=direct_recv, device_id=place(z, j), device_id_type=MESH)

    def mirror_copy(b, j):
        return pltpu.make_async_remote_copy(
            src_ref=sums.at[b], dst_ref=mirror.at[d, stripe], send_sem=mirror_send.at[b],
            recv_sem=mirror_recv, device_id=place(j, z), device_id_type=MESH)

    for b in range(1, rows):
        j = lax.rem(z - b + rows, rows)

        @pl.when(worked(rows, z, b))
        def _():
            first = jnp.where(held_upper(rows, z, b), acc_a[pl.ds(b * n, n), :], 0.0)
            second = jnp.where(held_lower(rows, z, rows - b), acc_b[pl.ds((rows - b) * n, n), :], 0.0)
            sums[b] = first + second
            mirror_copy(b, j).start()

            @pl.when(j != q)
            def _():
                direct_copy(b, j).start()

            @pl.when(j == q)
            def _():
                direct[d, stripe] = sums[b]

    sums[0] = acc_a[pl.ds(0, n), :] + acc_b[pl.ds(0, n), :]

    @pl.when(z != q)
    def _():
        mirror_copy(0, z).start()

    @pl.when(z == q)
    def _():
        mirror[d, stripe] = sums[0]

    def sent(block, sem):
        pltpu.make_async_copy(block, block, sem).wait()

    for b in range(rows - 1):
        @pl.when((b <= z) & (z < rows - 1) & jnp.logical_not((b == 0) & (z == rows - 2)))
        def _():
            sent(upper.at[pl.ds(b * n, n)], up_send.at[b])

        @pl.when((b <= m) & (m < rows - 1) & jnp.logical_not((b == 0) & (m == rows - 2)))
        def _():
            sent(lower.at[pl.ds(b * n, n)], down_send.at[b])

    @pl.when((z == 0) | (m == 0))
    def _():
        sent(upper.at[pl.ds(0, n)], extra_send)

    for rel in range(1, cols):
        sent(tile.at[own_rows], plane_send.at[rel])

    def received(buffer, recv, own):
        @pl.when(own)
        def _():
            others = sums.at[pl.ds(0, cols * depths - 1)]
            pltpu.make_async_copy(others, others, recv).wait()

        @pl.when(jnp.logical_not(own))
        def _():
            pltpu.make_async_copy(buffer, buffer, recv).wait()

    has_direct = (z != q) & worked(rows, z, lax.rem(z - q + rows, rows))
    has_mirror = (z == q) | worked(rows, q, lax.rem(q - z + rows, rows))

    def gathered(buffer):
        total = buffer[0]
        for dd in range(1, depths):
            total = total + buffer[dd]
        return total

    @pl.when(has_direct)
    def _():
        others = sums.at[pl.ds(0, cols * depths - 1)]
        pltpu.make_async_copy(others, others, direct_recv).wait()
        out[...] = gathered(direct).T

    @pl.when(has_mirror)
    def _():
        received(mirror, mirror_recv, z == q)
        total = gathered(mirror)

        @pl.when(has_direct)
        def _():
            out[...] += total

        @pl.when(jnp.logical_not(has_direct))
        def _():
            out[...] = total

    for b in range(rows):
        j = lax.rem(z - b + rows, rows)
        if b:
            @pl.when(worked(rows, z, b))
            def _():
                mirror_copy(b, j).wait_send()

                @pl.when(j != q)
                def _():
                    direct_copy(b, j).wait_send()
        else:
            @pl.when(z != q)
            def _():
                mirror_copy(0, z).wait_send()


def shards(rows, cols, depths, mantissa, exponent):
    n, features = mantissa.shape
    size = n * cols
    half = features // 2
    dma = pltpu.SemaphoreType.DMA
    return pl.pallas_call(
        functools.partial(kernel, rows, cols, depths),
        out_shape=jax.ShapeDtypeStruct((size, size), jnp.float32),
        in_specs=[pl.BlockSpec(memory_space=pltpu.HBM)] * 2,
        out_specs=pl.BlockSpec(memory_space=pltpu.VMEM),
        scratch_shapes=[
            pltpu.VMEM((n, features), jnp.bfloat16),
            pltpu.VMEM((n,), jnp.int32),
            pltpu.VMEM((size, features), jnp.bfloat16),
            pltpu.VMEM((rows * n, half), jnp.bfloat16),
            pltpu.VMEM((rows * n, half), jnp.bfloat16),
            pltpu.VMEM((rows * n, size), jnp.float32),
            pltpu.VMEM((rows * n, size), jnp.float32),
            pltpu.VMEM((rows, n, size), jnp.float32),
            pltpu.VMEM((depths, size, size), jnp.float32),
            pltpu.VMEM((depths, size, size), jnp.float32),
            dma((2, CHUNKS)), dma,
            dma((cols,)), dma((cols, 2 * PLANE)),
            dma((rows,)), dma((rows, CHUNKS)),
            dma((rows,)), dma((rows, CHUNKS)),
            dma,
            dma((rows,)), dma,
            dma((rows,)), dma,
        ],
        compiler_params=pltpu.CompilerParams(
            collective_id=0, has_side_effects=True, vmem_limit_bytes=63 * 2**20),
    )(mantissa, exponent)


def solution(mesh):
    rows, cols, depths = (mesh.shape[axis] for axis in ("row", "col", "depth"))
    assert rows >= 4 and cols & (cols - 1) == 0 and rows == cols * depths
    in_specs = (P(("groups", "row", "col"), "depth"), P(("groups", "row", "col")))
    out_specs = P(("groups", "row"), ("col", "depth"))
    return jax.shard_map(
        functools.partial(shards, rows, cols, depths), mesh=mesh, in_specs=in_specs, out_specs=out_specs, check_vma=False)
```

time: 32.3 us -> 28.6 us (0.89)
  the two profiles are of different devices: /device:TPU:0 before, /device:TPU:3 now
where the time goes in v2:
time: 28.6 us; the launch traced here: 28.4 us
  Pallas kernels  26.9 us (94%)
  local copies, waits for them, and re-layouts  1.47 us (5%)
    pallas_call x1, Pallas kernels, shards(): pl.pallas_call(functools.partial(kernel, rows, cols, depths), out_shape=j...  26.9 us
    unnamed x1, local copies, waits for them, and re-layouts  1.47 us

profile of v2, /device:TPU:3, one launch (start us, length us, event | category | flops | bytes accessed | tf_op | source)
XLA Modules:
  0.0 28.4 jit_solution(12177006723164274752)
XLA Ops:
  0.0 26.9 %shard_map.28 = f32[128,128]{1,0:T(8,128)} custom-call(bf16[32,8192]{1,0:T(8,128)(2,1)} %mantissa.1, s32[32]{0:T(128)} %exponent.1), custom_call_target="tpu_custom_call" | custom-call | tf_op jit(solution)/shard_map/pallas_call | solution.py:359
  26.9 1.5 %copy.4 = f32[128,128]{1,0:T(8,128)} copy(f32[128,128]{1,0:T(8,128)} %shard_map.28) | data formatting | bytes 131072

commit v3 on v2

--- a/solution.py
+++ b/solution.py
@@ -7,7 +7,8 @@
 from jax.experimental.pallas import tpu as pltpu
 from jax.sharding import PartitionSpec as P
 
-CHUNKS = 4
+PIECES = (4, 4, 4, 4)
+CHUNKS = len(PIECES)
 PLANE = 2
 LAG = 3
 MESH = pl.DeviceIdType.MESH
@@ -44,11 +45,12 @@
     n, features = raw.shape
     size = n * cols
     half = features // 2
-    width = half // CHUNKS
+    widths = [half * piece // sum(PIECES) for piece in PIECES]
+    starts = [sum(widths[:i]) for i in range(CHUNKS)]
     q = c * depths + d
 
     def load(half_index, i):
-        piece = pl.ds(half_index * half + i * width, width)
+        piece = pl.ds(half_index * half + starts[i], widths[i])
         return pltpu.make_async_copy(mantissa.at[:, piece], raw.at[:, piece], load_sem.at[half_index, i])
 
     for i in range(CHUNKS):
@@ -59,22 +61,15 @@
 
     barrier = pltpu.get_barrier_semaphore()
 
-    def greet(k, _):
-        @pl.when(k != q)
-        def _():
-            there = {"col": k // depths, "depth": k % depths}
-            pl.semaphore_signal(barrier, inc=1, device_id=there, device_id_type=MESH)
-
-        return 0
-
-    lax.fori_loop(0, cols * depths, greet, 0)
-
-    @pl.when(z > 0)
+    for k in range(cols):
+        for kk in range(depths):
+            if k or kk:
+                there = {"col": c ^ k, "depth": lax.rem(d + kk, depths)}
+                pl.semaphore_signal(barrier, inc=1, device_id=there, device_id_type=MESH)
+
+    @pl.when((z > 0) & (z < rows - 1))
     def _():
         pl.semaphore_signal(barrier, inc=1, device_id={"row": z - 1}, device_id_type=MESH)
-
-    @pl.when(z < rows - 1)
-    def _():
         pl.semaphore_signal(barrier, inc=1, device_id={"row": z + 1}, device_id_type=MESH)
 
     load_powers.wait()
@@ -85,16 +80,17 @@
 
     def scaled(half_index, i, block):
         load(half_index, i).wait()
-        piece = pl.ds(half_index * half + i * width, width)
+        piece = pl.ds(half_index * half + starts[i], widths[i])
         value = (raw[:, piece].astype(jnp.float32) * scale).astype(jnp.bfloat16)
         tile[own_rows, piece] = value
-        block[pl.ds(0, n), pl.ds(i * width, width)] = value
-
-    span = half // PLANE
+        block[pl.ds(0, n), pl.ds(starts[i], widths[i])] = value
+
+    per_span = CHUNKS // PLANE
 
     def plane_block(rel, t):
-        start = t % 2 * half + t // 2 * span
-        return tile.at[pl.ds(pl.multiple_of((c ^ rel) * n, n), n), pl.ds(start, span)]
+        first = t // 2 * per_span
+        columns = pl.ds(t % 2 * half + starts[first], sum(widths[first : first + per_span]))
+        return tile.at[pl.ds(pl.multiple_of((c ^ rel) * n, n), n), columns]
 
     def plane_copy(rel, bit, t):
         block = plane_block(rel, t)
@@ -117,19 +113,19 @@
                     plane_copy(rel, low, t).start()
 
     def line_copy(buffer, send, recv, there, b, i):
-        piece = pl.ds(i * width, width)
+        piece = pl.ds(starts[i], widths[i])
         return pltpu.make_async_remote_copy(
             src_ref=buffer.at[pl.ds(b * n, n), piece], dst_ref=buffer.at[pl.ds((b + 1) * n, n), piece],
             send_sem=send.at[b], recv_sem=recv.at[b + 1, i], device_id={"row": there}, device_id_type=MESH)
 
     def extra_copy(buffer, recv, there, i):
-        piece = pl.ds(i * width, width)
+        piece = pl.ds(starts[i], widths[i])
         return pltpu.make_async_remote_copy(
             src_ref=buffer.at[pl.ds(0, n), piece], dst_ref=buffer.at[pl.ds((rows - 1) * n, n), piece],
             send_sem=extra_send, recv_sem=recv.at[rows - 1, i], device_id={"row": there}, device_id_type=MESH)
 
     def line_arrived(buffer, recv, b, i):
-        block = buffer.at[pl.ds(b * n, n), pl.ds(i * width, width)]
+        block = buffer.at[pl.ds(b * n, n), pl.ds(starts[i], widths[i])]
         pltpu.make_async_copy(block, block, recv.at[b, i]).wait()
 
     m = rows - 1 - z
@@ -158,21 +154,31 @@
         b, i = divmod(t, CHUNKS)
         b += 1
 
-        @pl.when((b <= z) & (z <= rows - 2))
-        def _():
+        @pl.when(z == rows - 2)
+        def _():
+            if t == 0:
+                line_arrived(lower, down_recv, b, i)
             line_arrived(upper, up_recv, b, i)
-
-            @pl.when(z == rows - 2)
-            def _():
-                line_copy(upper, up_send, up_recv, z + 1, b, i).start()
-
-        @pl.when((b <= m) & (m <= rows - 2))
-        def _():
+            line_copy(upper, up_send, up_recv, z + 1, b, i).start()
+            if b == 1 and t:
+                line_arrived(lower, down_recv, b, i)
+
+        @pl.when(m == rows - 2)
+        def _():
+            if t == 0:
+                line_arrived(upper, up_recv, b, i)
             line_arrived(lower, down_recv, b, i)
-
-            @pl.when(m == rows - 2)
-            def _():
-                line_copy(lower, down_send, down_recv, z - 1, b, i).start()
+            line_copy(lower, down_send, down_recv, z - 1, b, i).start()
+            if b == 1 and t:
+                line_arrived(upper, up_recv, b, i)
+
+        @pl.when((z > 1) & (b <= z) & (z < rows - 2))
+        def _():
+            line_arrived(upper, up_recv, b, i)
+
+        @pl.when((m > 1) & (b <= m) & (m < rows - 2))
+        def _():
+            line_arrived(lower, down_recv, b, i)
 
     def last_arrivals(i):
         @pl.when(z == rows - 2)
@@ -196,7 +202,7 @@
     dims = (((1,), (1,)), ((), ()))
 
     def multiply(i):
-        piece, other = pl.ds(i * width, width), pl.ds(half + i * width, width)
+        piece, other = pl.ds(starts[i], widths[i]), pl.ds(half + starts[i], widths[i])
         term_a = lax.dot_general(upper[:, piece], tile[:, piece], dims, preferred_element_type=jnp.float32)
         term_b = lax.dot_general(lower[:, piece], tile[:, other], dims, preferred_element_type=jnp.float32)
         if i == 0:
@@ -213,10 +219,9 @@
             scaled(0, step, upper)
             scaled(1, step, lower)
         if step == 0:
-            pl.semaphore_wait(barrier, cols * depths + 1 - jnp.where((z == 0) | (z == rows - 1), 1, 0))
+            pl.semaphore_wait(barrier, cols * depths + jnp.where((z >= 2) & (z <= rows - 3), 1, 0))
         if step < line_steps:
             line_sends(step)
-        per_span = CHUNKS // PLANE
         if step < CHUNKS and step % per_span == per_span - 1:
             for t in (step // per_span * 2, step // per_span * 2 + 1):
                 for bit in lower_bits(0):
@@ -232,8 +237,16 @@
                 plane_arrivals(t)
             plane_done = due
             if i >= 0:
-                last_arrivals(i)
-                multiply(i)
+                @pl.when((z == 0) | (m == 0))
+                def _():
+                    last_arrivals(i)
+                    multiply(i)
+
+    @pl.when((z > 0) & (m > 0))
+    def _():
+        for i in range(CHUNKS):
+            last_arrivals(i)
+            multiply(i)
 
     def place(row, tile_index):
         return {"row": row, "col": tile_index // depths, "depth": tile_index % depths}
@@ -250,7 +263,8 @@
             src_ref=sums.at[b], dst_ref=mirror.at[d, stripe], send_sem=mirror_send.at[b],
             recv_sem=mirror_recv, device_id=place(j, z), device_id_type=MESH)
 
-    for b in range(1, rows):
+
+    for b in reversed(range(1, rows)):
         j = lax.rem(z - b + rows, rows)
 
         @pl.when(worked(rows, z, b))
@@ -260,14 +274,6 @@
             sums[b] = first + second
             mirror_copy(b, j).start()
 
-            @pl.when(j != q)
-            def _():
-                direct_copy(b, j).start()
-
-            @pl.when(j == q)
-            def _():
-                direct[d, stripe] = sums[b]
-
     sums[0] = acc_a[pl.ds(0, n), :] + acc_b[pl.ds(0, n), :]
 
     @pl.when(z != q)
@@ -277,6 +283,17 @@
     @pl.when(z == q)
     def _():
         mirror[d, stripe] = sums[0]
+
+    for b in range(1, rows):
+        j = lax.rem(z - b + rows, rows)
+
+        @pl.when(worked(rows, z, b) & (j != q))
+        def _():
+            direct_copy(b, j).start()
+
+        @pl.when(worked(rows, z, b) & (j == q))
+        def _():
+            direct[d, stripe] = sums[b]
 
     def sent(block, sem):
         pltpu.make_async_copy(block, block, sem).wait()

time: 28.6 us -> 27.1 us (0.948)
  the two profiles are of different devices: /device:TPU:3 before, /device:TPU:0 now
where the time goes in v3:
time: 27.1 us; the launch traced here: 26.8 us
  Pallas kernels  25.3 us (93%)
  local copies, waits for them, and re-layouts  1.47 us (5%)
    pallas_call x1, Pallas kernels, shards(): pl.pallas_call(functools.partial(kernel, rows, cols, depths), out_shape=j...  25.3 us
    unnamed x1, local copies, waits for them, and re-layouts  1.47 us

profile of v3, /device:TPU:0, one launch (start us, length us, event | category | flops | bytes accessed | tf_op | source)
XLA Modules:
  0.0 26.8 jit_solution(14973681511124070847)
XLA Ops:
  0.0 25.3 %shard_map.28 = f32[128,128]{1,0:T(8,128)} custom-call(bf16[32,8192]{1,0:T(8,128)(2,1)} %mantissa.1, s32[32]{0:T(128)} %exponent.1), custom_call_target="tpu_custom_call" | custom-call | tf_op jit(solution)/shard_map/pallas_call | solution.py:376
  25.3 1.5 %copy.4 = f32[128,128]{1,0:T(8,128)} copy(f32[128,128]{1,0:T(8,128)} %shard_map.28) | data formatting | bytes 131072

commit v4 on v3

--- a/solution.py
+++ b/solution.py
@@ -11,6 +11,7 @@
 CHUNKS = len(PIECES)
 PLANE = 2
 LAG = 3
+LAST = CHUNKS - 1
 MESH = pl.DeviceIdType.MESH
 
 
@@ -39,7 +40,7 @@
 
 
 def kernel(rows, cols, depths, mantissa, exponent, out, raw, powers, tile, upper, lower, acc_a, acc_b, sums, direct, mirror,
-           load_sem, power_sem, plane_send, plane_recv, up_send, up_recv, down_send, down_recv, extra_send,
+           load_sem, power_sem, plane_send, plane_recv, up_send, up_recv, down_send, down_recv, extra_send, beyond_send,
            direct_send, direct_recv, mirror_send, mirror_recv):
     z, c, d = lax.axis_index("row"), lax.axis_index("col"), lax.axis_index("depth")
     n, features = raw.shape
@@ -133,22 +134,50 @@
     def line_sends(t):
         b, i = divmod(t, CHUNKS)
 
-        @pl.when((z < rows - 2) & (b <= z))
+        late = t == LAST
+
+        @pl.when((z < rows - 2 - late) & (b <= z))
         def _():
             line_copy(upper, up_send, up_recv, z + 1, b, i).start()
 
-        @pl.when((m < rows - 2) & (b <= m))
+        @pl.when((m < rows - 2 - late) & (b <= m))
         def _():
             line_copy(lower, down_send, down_recv, z - 1, b, i).start()
 
         if b == 1:
             @pl.when(z == 0)
             def _():
-                extra_copy(lower, down_recv, z + 1, i).start()
+                extra_copy(lower, down_recv, z + 1, (i + LAST) % CHUNKS).start()
 
             @pl.when(m == 0)
             def _():
-                extra_copy(upper, up_recv, z - 1, i).start()
+                extra_copy(upper, up_recv, z - 1, (i + LAST) % CHUNKS).start()
+
+    def late_sends():
+        @pl.when(z == rows - 3)
+        def _():
+            line_copy(upper, up_send, up_recv, z + 1, 0, LAST).start()
+
+        @pl.when(m == rows - 3)
+        def _():
+            line_copy(lower, down_send, down_recv, z - 1, 0, LAST).start()
+
+    def beyond_copy(buffer, recv, there):
+        piece = pl.ds(starts[LAST], widths[LAST])
+        return pltpu.make_async_remote_copy(
+            src_ref=buffer.at[pl.ds((rows - 1) * n, n), piece], dst_ref=buffer.at[pl.ds((rows - 2) * n, n), piece],
+            send_sem=beyond_send, recv_sem=recv.at[rows - 2, LAST], device_id={"row": there}, device_id_type=MESH)
+
+    def beyond_sends():
+        @pl.when(z == 1)
+        def _():
+            line_arrived(lower, down_recv, rows - 1, LAST)
+            beyond_copy(lower, down_recv, z + 1).start()
+
+        @pl.when(m == 1)
+        def _():
+            line_arrived(upper, up_recv, rows - 1, LAST)
+            beyond_copy(upper, up_recv, z - 1).start()
 
     def line_arrivals(t):
         b, i = divmod(t, CHUNKS)
@@ -158,8 +187,9 @@
         def _():
             if t == 0:
                 line_arrived(lower, down_recv, b, i)
-            line_arrived(upper, up_recv, b, i)
-            line_copy(upper, up_send, up_recv, z + 1, b, i).start()
+            if t != LAST:
+                line_arrived(upper, up_recv, b, i)
+                line_copy(upper, up_send, up_recv, z + 1, b, i).start()
             if b == 1 and t:
                 line_arrived(lower, down_recv, b, i)
 
@@ -167,8 +197,9 @@
         def _():
             if t == 0:
                 line_arrived(upper, up_recv, b, i)
-            line_arrived(lower, down_recv, b, i)
-            line_copy(lower, down_send, down_recv, z - 1, b, i).start()
+            if t != LAST:
+                line_arrived(lower, down_recv, b, i)
+                line_copy(lower, down_send, down_recv, z - 1, b, i).start()
             if b == 1 and t:
                 line_arrived(upper, up_recv, b, i)
 
@@ -181,23 +212,20 @@
             line_arrived(lower, down_recv, b, i)
 
     def last_arrivals(i):
-        @pl.when(z == rows - 2)
-        def _():
-            line_arrived(upper, up_recv, rows - 1, i)
-
-        @pl.when(m == rows - 2)
-        def _():
-            line_arrived(lower, down_recv, rows - 1, i)
-
-        @pl.when(z == rows - 1)
-        def _():
-            for b in range(2, rows):
-                line_arrived(upper, up_recv, b, i)
-
-        @pl.when(m == rows - 1)
-        def _():
-            for b in range(2, rows):
-                line_arrived(lower, down_recv, b, i)
+        for at, buffer, recv in ((m, upper, up_recv), (z, lower, down_recv)):
+            @pl.when(at == 0)
+            def _():
+                for b in range(3 if i == LAST else 2, rows):
+                    line_arrived(buffer, recv, b, i)
+
+            @pl.when(at == 1)
+            def _():
+                line_arrived(buffer, recv, 1 if i == LAST else rows - 1, i)
+
+            if i == LAST:
+                @pl.when(at == 2)
+                def _():
+                    line_arrived(buffer, recv, rows - 2, i)
 
     dims = (((1,), (1,)), ((), ()))
 
@@ -205,6 +233,13 @@
         piece, other = pl.ds(starts[i], widths[i]), pl.ds(half + starts[i], widths[i])
         term_a = lax.dot_general(upper[:, piece], tile[:, piece], dims, preferred_element_type=jnp.float32)
         term_b = lax.dot_general(lower[:, piece], tile[:, other], dims, preferred_element_type=jnp.float32)
+        block = lax.broadcasted_iota(jnp.int32, (rows * n, size), 0) // n
+        if i == LAST:
+            term_a = jnp.where((m == 0) & (block == 2), 0.0, term_a)
+            term_b = jnp.where((z == 0) & (block == 2), 0.0, term_b)
+        else:
+            term_a = jnp.where((m == 2) & (block == rows - 2), 0.0, term_a)
+            term_b = jnp.where((z == 2) & (block == rows - 2), 0.0, term_b)
         if i == 0:
             acc_a[...] = term_a
             acc_b[...] = term_b
@@ -222,6 +257,8 @@
             pl.semaphore_wait(barrier, cols * depths + jnp.where((z >= 2) & (z <= rows - 3), 1, 0))
         if step < line_steps:
             line_sends(step)
+        if step == line_steps - 1:
+            late_sends()
         if step < CHUNKS and step % per_span == per_span - 1:
             for t in (step // per_span * 2, step // per_span * 2 + 1):
                 for bit in lower_bits(0):
@@ -229,6 +266,9 @@
         done = step - LAG
         if done >= 0:
             line_arrivals(done)
+        if step == line_steps:
+            beyond_sends()
+        if done >= 0:
             i = done - (rows - 3) * CHUNKS
             due = min((done + 1) // per_span, 2 * PLANE)
             if i >= 0:
@@ -269,8 +309,8 @@
 
         @pl.when(worked(rows, z, b))
         def _():
-            first = jnp.where(held_upper(rows, z, b), acc_a[pl.ds(b * n, n), :], 0.0)
-            second = jnp.where(held_lower(rows, z, rows - b), acc_b[pl.ds((rows - b) * n, n), :], 0.0)
+            first = jnp.where(held_upper(rows, z, b) | ((m == 2) & (b == rows - 2)), acc_a[pl.ds(b * n, n), :], 0.0)
+            second = jnp.where(held_lower(rows, z, rows - b) | ((z == 2) & (b == 2)), acc_b[pl.ds((rows - b) * n, n), :], 0.0)
             sums[b] = first + second
             mirror_copy(b, j).start()
 
@@ -299,13 +339,19 @@
         pltpu.make_async_copy(block, block, sem).wait()
 
     for b in range(rows - 1):
-        @pl.when((b <= z) & (z < rows - 1) & jnp.logical_not((b == 0) & (z == rows - 2)))
-        def _():
-            sent(upper.at[pl.ds(b * n, n)], up_send.at[b])
-
-        @pl.when((b <= m) & (m < rows - 1) & jnp.logical_not((b == 0) & (m == rows - 2)))
-        def _():
-            sent(lower.at[pl.ds(b * n, n)], down_send.at[b])
+        for at, buffer, send in ((z, upper, up_send), (m, lower, down_send)):
+            @pl.when((b <= at) & (at < rows - 2))
+            def _():
+                sent(buffer.at[pl.ds(b * n, n)], send.at[b])
+
+            if b:
+                @pl.when(at == rows - 2)
+                def _():
+                    sent(buffer.at[pl.ds(b * n, n), pl.ds(0, starts[LAST] if b == 1 else half)], send.at[b])
+
+    @pl.when((z == 1) | (m == 1))
+    def _():
+        sent(upper.at[pl.ds(0, n), pl.ds(starts[LAST], widths[LAST])], beyond_send)
 
     @pl.when((z == 0) | (m == 0))
     def _():
@@ -393,7 +439,7 @@
             dma((cols,)), dma((cols, 2 * PLANE)),
             dma((rows,)), dma((rows, CHUNKS)),
             dma((rows,)), dma((rows, CHUNKS)),
-            dma,
+            dma, dma,
             dma((rows,)), dma,
             dma((rows,)), dma,
         ],

time: 27.1 us -> 26.9 us (level)
  no operation moved by 1% of the time
where the time goes in v4:
time: 26.9 us; the launch traced here: 26.7 us
  Pallas kernels  25.3 us (94%)
  local copies, waits for them, and re-layouts  1.47 us (5%)
    pallas_call x1, Pallas kernels, shards(): pl.pallas_call(functools.partial(kernel, rows, cols, depths), out_shape=j...  25.3 us
    unnamed x1, local copies, waits for them, and re-layouts  1.47 us

profile of v4, /device:TPU:0, one launch (start us, length us, event | category | flops | bytes accessed | tf_op | source)
XLA Modules:
  0.0 26.7 jit_solution(13777850873991895572)
XLA Ops:
  0.0 25.3 %shard_map.28 = f32[128,128]{1,0:T(8,128)} custom-call(bf16[32,8192]{1,0:T(8,128)(2,1)} %mantissa.1, s32[32]{0:T(128)} %exponent.1), custom_call_target="tpu_custom_call" | custom-call | tf_op jit(solution)/shard_map/pallas_call | solution.py:422
  25.3 1.5 %copy.4 = f32[128,128]{1,0:T(8,128)} copy(f32[128,128]{1,0:T(8,128)} %shard_map.28) | data formatting | bytes 131072

commit v5 on v4

--- a/solution.py
+++ b/solution.py
@@ -87,10 +87,13 @@
         block[pl.ds(0, n), pl.ds(starts[i], widths[i])] = value
 
     per_span = CHUNKS // PLANE
+    span = half // PLANE
 
     def plane_block(rel, t):
-        first = t // 2 * per_span
-        columns = pl.ds(t % 2 * half + starts[first], sum(widths[first : first + per_span]))
+        upper_first, lower_first = t * span, (t + PLANE) % (2 * PLANE) * span
+        by_turns = t % 2 * half + t // 2 * span
+        start = jnp.where(z == 0, lower_first, jnp.where(z == rows - 1, upper_first, by_turns))
+        columns = pl.ds(pl.multiple_of(start, span), span)
         return tile.at[pl.ds(pl.multiple_of((c ^ rel) * n, n), n), columns]
 
     def plane_copy(rel, bit, t):
@@ -105,13 +108,20 @@
             yield bit
             bit >>= 1
 
-    def plane_arrivals(t):
-        for bit in reversed(range(cols.bit_length() - 1)):
+    def plane_wait(rel, t):
+        block = plane_block(rel, t)
+        pltpu.make_async_copy(block, block, plane_recv.at[rel, t]).wait()
+
+    def plane_pass(t):
+        for bit in reversed(range(1, cols.bit_length() - 1)):
             for rel in range(1 << bit, cols, 1 << (bit + 1)):
-                block = plane_block(rel, t)
-                pltpu.make_async_copy(block, block, plane_recv.at[rel, t]).wait()
+                plane_wait(rel, t)
                 for low in lower_bits(rel):
                     plane_copy(rel, low, t).start()
+
+    def plane_rest(t):
+        for rel in range(1, cols, 2):
+            plane_wait(rel, t)
 
     def line_copy(buffer, send, recv, there, b, i):
         piece = pl.ds(starts[i], widths[i])
@@ -229,23 +239,26 @@
 
     dims = (((1,), (1,)), ((), ()))
 
-    def multiply(i):
-        piece, other = pl.ds(starts[i], widths[i]), pl.ds(half + starts[i], widths[i])
-        term_a = lax.dot_general(upper[:, piece], tile[:, piece], dims, preferred_element_type=jnp.float32)
-        term_b = lax.dot_general(lower[:, piece], tile[:, other], dims, preferred_element_type=jnp.float32)
-        block = lax.broadcasted_iota(jnp.int32, (rows * n, size), 0) // n
+    block = lax.broadcasted_iota(jnp.int32, (rows * n, size), 0) // n
+
+    def add(acc, features_of, offset, at, i):
+        term = lax.dot_general(
+            features_of[:, pl.ds(starts[i], widths[i])], tile[:, pl.ds(offset + starts[i], widths[i])], dims,
+            preferred_element_type=jnp.float32)
         if i == LAST:
-            term_a = jnp.where((m == 0) & (block == 2), 0.0, term_a)
-            term_b = jnp.where((z == 0) & (block == 2), 0.0, term_b)
+            term = jnp.where((at == 0) & (block == 2), 0.0, term)
         else:
-            term_a = jnp.where((m == 2) & (block == rows - 2), 0.0, term_a)
-            term_b = jnp.where((z == 2) & (block == rows - 2), 0.0, term_b)
+            term = jnp.where((at == 2) & (block == rows - 2), 0.0, term)
         if i == 0:
-            acc_a[...] = term_a
-            acc_b[...] = term_b
+            acc[...] = term
         else:
-            acc_a[...] += term_a
-            acc_b[...] += term_b
+            acc[...] += term
+
+    def multiply_upper(i):
+        add(acc_a, upper, 0, m, i)
+
+    def multiply_lower(i):
+        add(acc_b, lower, half, z, i)
 
     line_steps = (rows - 2) * CHUNKS
     plane_done = 0
@@ -259,8 +272,8 @@
             line_sends(step)
         if step == line_steps - 1:
             late_sends()
-        if step < CHUNKS and step % per_span == per_span - 1:
-            for t in (step // per_span * 2, step // per_span * 2 + 1):
+        if step in (per_span - 1, CHUNKS - 1):
+            for t in range(1) if step < CHUNKS - 1 else range(1, 2 * PLANE):
                 for bit in lower_bits(0):
                     plane_copy(0, bit, t).start()
         done = step - LAG
@@ -269,24 +282,34 @@
         if step == line_steps:
             beyond_sends()
         if done >= 0:
+            due = min((done + 1) // per_span, 2 * PLANE)
+            for t in range(plane_done, due):
+                plane_pass(t)
+            plane_done = due
             i = done - (rows - 3) * CHUNKS
-            due = min((done + 1) // per_span, 2 * PLANE)
-            if i >= 0:
-                due = max(due, i // per_span * 2 + 2)
-            for t in range(plane_done, due):
-                plane_arrivals(t)
-            plane_done = due
             if i >= 0:
                 @pl.when((z == 0) | (m == 0))
                 def _():
+                    if i % per_span == 0:
+                        plane_rest(i // per_span)
                     last_arrivals(i)
-                    multiply(i)
+
+                @pl.when(z == 0)
+                def _():
+                    multiply_lower(i)
+
+                @pl.when(m == 0)
+                def _():
+                    multiply_upper(i)
 
     @pl.when((z > 0) & (m > 0))
     def _():
+        for t in range(2 * PLANE):
+            plane_rest(t)
         for i in range(CHUNKS):
             last_arrivals(i)
-            multiply(i)
+            multiply_upper(i)
+            multiply_lower(i)
 
     def place(row, tile_index):
         return {"row": row, "col": tile_index // depths, "depth": tile_index % depths}
@@ -314,16 +337,6 @@
             sums[b] = first + second
             mirror_copy(b, j).start()
 
-    sums[0] = acc_a[pl.ds(0, n), :] + acc_b[pl.ds(0, n), :]
-
-    @pl.when(z != q)
-    def _():
-        mirror_copy(0, z).start()
-
-    @pl.when(z == q)
-    def _():
-        mirror[d, stripe] = sums[0]
-
     for b in range(1, rows):
         j = lax.rem(z - b + rows, rows)
 
@@ -334,6 +347,31 @@
         @pl.when(worked(rows, z, b) & (j == q))
         def _():
             direct[d, stripe] = sums[b]
+
+    for i in range(CHUNKS):
+        @pl.when((z == 0) | (m == 0))
+        def _():
+            if i % per_span == 0:
+                plane_rest(PLANE + i // per_span)
+
+        piece = pl.ds(starts[i], widths[i])
+        for at, acc, features_of, offset in ((z, acc_a, upper, 0), (m, acc_b, lower, half)):
+            @pl.when(at == 0)
+            def _():
+                term = lax.dot_general(
+                    features_of[pl.ds(0, n), piece], tile[:, pl.ds(offset + starts[i], widths[i])], dims,
+                    preferred_element_type=jnp.float32)
+                acc[pl.ds(0, n), :] = term if i == 0 else acc[pl.ds(0, n), :] + term
+
+    sums[0] = acc_a[pl.ds(0, n), :] + acc_b[pl.ds(0, n), :]
+
+    @pl.when(z != q)
+    def _():
+        mirror_copy(0, z).start()
+
+    @pl.when(z == q)
+    def _():
+        mirror[d, stripe] = sums[0]
 
     def sent(block, sem):
         pltpu.make_async_copy(block, block, sem).wait()

time: 26.9 us -> 27 us (level)
  no operation moved by 1% of the time
where the time goes in v5:
time: 27 us; the launch traced here: 26.8 us
  Pallas kernels  25.3 us (94%)
  local copies, waits for them, and re-layouts  1.47 us (5%)
    pallas_call x1, Pallas kernels, shards(): pl.pallas_call(functools.partial(kernel, rows, cols, depths), out_shape=j...  25.3 us
    unnamed x1, local copies, waits for them, and re-layouts  1.47 us

profile of v5, /device:TPU:0, one launch (start us, length us, event | category | flops | bytes accessed | tf_op | source)
XLA Modules:
  0.0 26.8 jit_solution(14226431202341178585)
XLA Ops:
  0.0 25.3 %shard_map.28 = f32[128,128]{1,0:T(8,128)} custom-call(bf16[32,8192]{1,0:T(8,128)(2,1)} %mantissa.1, s32[32]{0:T(128)} %exponent.1), custom_call_target="tpu_custom_call" | custom-call | tf_op jit(solution)/shard_map/pallas_call | solution.py:460
  25.3 1.5 %copy.4 = f32[128,128]{1,0:T(8,128)} copy(f32[128,128]{1,0:T(8,128)} %shard_map.28) | data formatting | bytes 131072
